TPU v7x, 256 devices: a whole 4x4x8 slice. The times are simulated.
256 devices in a mesh: seq: 8 (over x, core), expert: 32 (over z, y).
Axes of the slice: x: 4, y: 4, z: 8, core: 2. Of those that a mesh axis runs over, the one named last changes fastest.
Arguments:
- tokens: bfloat16 [8192, 2048], P('expert'), may hold values from -6 to 6
- routes: int32 [8192, 6], P('expert'), may hold values from 0 to 63, all different within a row; in each aligned block of 256 rows (0 to 255, 256 to 511, ...) at most 32 rows name the same one
- gates: float32 [8192, 6], P('expert'), may hold values from 0.05 to 0.5
- expert_gate: bfloat16 [64, 2048, 1408], P('expert', None, 'seq'), may hold values from -0.125 to 0.125
- expert_up: bfloat16 [64, 2048, 1408], P('expert', None, 'seq'), may hold values from -0.125 to 0.125
- expert_down: bfloat16 [64, 1408, 2048], P('expert', 'seq'), may hold values from -0.15625 to 0.15625
- shared_gate: bfloat16 [2048, 2816], P(None, 'seq'), may hold values from -0.125 to 0.125
- shared_up: bfloat16 [2048, 2816], P(None, 'seq'), may hold values from -0.125 to 0.125
- shared_down: bfloat16 [2816, 2048], P('seq'), may hold values from -0.109375 to 0.109375
Outputs:
- mixed: bfloat16 [8192, 2048], P('expert', 'seq')
Inputs may be any that keep to these rules, and one draw needn't show every extreme that they name: `routes`: in each aligned block of 256 rows no expert is named by more than 32 rows, a bound that some block reaches; the numbers in one row differ.
All inputs are finite; a program needn't handle non-finite values.
Results may differ from a plain program's by a relative error of at most 0.02.
Values may be sent and summed in bfloat16 or wider, within the bound.
A program may use at most 128 MiB of HBM per device.

v0:
```python
import jax
import jax.numpy as jnp
from jax import lax
from jax.sharding import PartitionSpec as P


def slot_tables(routes, gates, experts, capacity):
    rows, top = routes.shape
    flat = routes.reshape(-1)
    onehot = (flat[:, None] == jnp.arange(experts, dtype=jnp.int32)[None, :]).astype(jnp.int32)
    before = jnp.cumsum(onehot, axis=0) - onehot
    rank = jnp.sum(before * onehot, axis=1)
    token_of = jnp.arange(rows * top, dtype=jnp.int32) // top
    slot_tok = jnp.zeros((experts, capacity), jnp.int32).at[flat, rank].set(token_of)
    slot_gate = jnp.zeros((experts, capacity), jnp.float32).at[flat, rank].set(gates.reshape(-1))
    return (slot_tok, slot_gate)


def shards(
    tokens, routes, gates, expert_gate, expert_up, expert_down, shared_gate, shared_up, shared_down
):
    rows, width = tokens.shape
    top = routes.shape[1]
    local_experts = expert_gate.shape[0]
    experts = local_experts * lax.axis_size("expert")
    capacity = rows * top * 4 // (3 * experts)
    slot_tok, slot_gate = slot_tables(routes, gates, experts, capacity)
    outgoing = tokens[slot_tok.reshape(-1)].reshape(experts, capacity, width)
    arrived = lax.all_to_all(outgoing, "expert", split_axis=0, concat_axis=1, tiled=True)
    gate = jnp.einsum("erd,edf->erf", arrived, expert_gate, preferred_element_type=jnp.float32)
    up = jnp.einsum("erd,edf->erf", arrived, expert_up, preferred_element_type=jnp.float32)
    hidden = (jax.nn.silu(gate) * up).astype(jnp.bfloat16)
    partial_value = jnp.einsum(
        "erf,efd->erd", hidden, expert_down, preferred_element_type=jnp.float32
    )
    partial_value = partial_value.astype(jnp.bfloat16)
    sgate = jnp.dot(tokens, shared_gate, preferred_element_type=jnp.float32)
    sup = jnp.dot(tokens, shared_up, preferred_element_type=jnp.float32)
    shidden = (jax.nn.silu(sgate) * sup).astype(jnp.bfloat16)
    shared_part = jnp.dot(shidden, shared_down, preferred_element_type=jnp.float32)
    flat_slots = slot_tok.reshape(-1)
    widened = lax.optimization_barrier(partial_value).astype(jnp.float32)
    summed = lax.psum_scatter(
        widened.astype(jnp.bfloat16), "seq", scatter_dimension=2, tiled=True
    ).astype(jnp.float32)
    returned = lax.all_to_all(
        summed.astype(jnp.bfloat16), "expert", split_axis=1, concat_axis=0, tiled=True
    ).astype(summed.dtype)
    columns = returned.shape[2]
    weighted = (slot_gate[:, :, None] * returned).reshape(-1, columns)
    routed = jnp.zeros((rows, columns), jnp.float32).at[flat_slots].add(weighted)
    shared = lax.psum_scatter(
        shared_part.astype(jnp.bfloat16), "seq", scatter_dimension=1, tiled=True
    ).astype(jnp.float32)
    mixed = routed + shared
    return mixed.astype(jnp.bfloat16)


def solution(mesh):
    return jax.shard_map(
        shards,
        mesh=mesh,
        in_specs=(
            P("expert", None),
            P("expert", None),
            P("expert", None),
            P("expert", None, "seq"),
            P("expert", None, "seq"),
            P("expert", "seq", None),
            P(None, "seq"),
            P(None, "seq"),
            P("seq", None),
        ),
        out_specs=P("expert", "seq"),
        check_vma=False,
    )
```

profile of v0, /device:TPU:6, one launch (start us, length us, event | category | flops | bytes accessed | tf_op | source)
XLA Modules:
  0.0 387.1 jit_solution(9459374887289010803)
XLA Ops:
  6.5 0.9 copy.29
  7.8 0.7 reshape.108
  8.5 0.6 add_select_fusion
  9.2 18.1 %reduce-window.6 = s32[64,12,128]{2,1,0:T(8,128)S(1)} reduce-window(s32[64,12,128]{2,1,0:T(8,128)S(1)} %fusion.3, s32[]{:T(128)} %constant.10.clone.1), window={size=1x1x128 pad=0_0x0_0x127_0}, to_apply=%region_1.2 | reduce-window | flops 12484608 | bytes 786436 | tf_op jit(solution)/shard_map/reduce-window
  27.5 0.3 copy.32
  28.8 6.3 %scatter_custom_fusion.1 = s32[2048]{0:T(1024)S(1)} fusion(s32[1536]{0:T(1024)S(1)} %broadcast_select_fusion, s32[1536]{0:T(1024)} %add_select_fusion, s32[]{:T(128)} %constant.10.clone.1), kind=kCustom, calls=%fused_computation.42 | custom fusion | bytes 8704
  35.4 11.0 %gather_fusion = bf16[2048,2048]{1,0:T(8,128)(2,1)} fusion(bf16[256,2048]{1,0:T(8,128)(2,1)S(1)} %copy-done.1, s32[2048]{0:T(1024)S(1)} %broadcast_clamp_fusion), kind=kCustom, calls=%fused_computation | custom fusion | bytes 16785408 | tf_op jit(solution)/shard_map/gather | solution.py:28
  46.4 197.0 %all_to_all.27 = bf16[64,32,2048]{2,1,0:T(8,128)(2,1)} all-to-all(bf16[64,32,2048]{2,1,0:T(8,128)(2,1)} %bitcast.43), channel_id=1, replica_groups=mesh['seq'=8,'expert'=32] {'expert'}, dimensions={0} | all-to-all | bytes 16777216 | tf_op jit(solution)/shard_map/all_to_all | solution.py:29
  243.4 8.4 %copy.37 = bf16[2,32,32,2048]{3,2,1,0:T(8,128)(2,1)} copy(bf16[2,32,32,2048]{3,2,0,1:T(8,128)(2,1)} %bitcast.46) | data formatting | bytes 16777216 | tf_op jit(solution)/shard_map/all_to_all | solution.py:29
  251.8 7.4 %fusion.23 = f32[2,1024,176]{1,2,0:T(8,128)} fusion(bf16[2,1024,2048]{2,1,0:T(8,128)(2,1)} %bitcast.44, bf16[2,2048,176]{1,2,0:T(8,128)(2,1)S(1)} %copy-done.2), kind=kOutput, calls=%fused_computation.48 | convolution fusion | flops 1476395008 | bytes 11272192 | tf_op jit(solution)/shard_map/erd,edf->erf/dot_general | solution.py:30
  259.2 14.3 %convolution_convert_fusion = bf16[2,1024,2048]{2,1,0:T(8,128)(2,1)} fusion(bf16[2,176,2048]{2,1,0:T(8,128)(2,1)S(1)} %copy-done, bf16[2,1024,2048]{2,1,0:T(8,128)(2,1)} %bitcast.45, bf16[2,2048,176]{1,2,0:T(8,128)(2,1)} %param.13, f32[2,1024,176]{1,2,0:T(8,128)} %fusion.23), kind=kOutput, calls=%fused_computation.4 | convolution fusion | flops 2959147008 | bytes 21102592 | tf_op jit(solution)/shard_map/erf,efd->erd/dot_general | solution.py:33
  273.8 1.9 fusion.22
  275.7 4.8 %convolution_convert_fusion.1 = bf16[256,2048]{1,0:T(8,128)(2,1)} fusion(bf16[352,2048]{1,0:T(8,128)(2,1)} %param.17, bf16[256,2048]{1,0:T(8,128)(2,1)S(1)} %copy-done.1, bf16[2048,352]{0,1:T(8,128)(2,1)} %param.16, f32[256,352]{0,1:T(8,128)S(1)} %fusion.22), kind=kOutput, calls=%fused_computation.5 | convolution fusion | flops 739262464 | bytes 5341184 | tf_op jit(solution)/shard_map/dot_general | solution.py:40
  280.6 43.2 %reduce-scatter.5.cloned.1.call-done = bf16[2,1024,256]{2,1,0:T(8,128)(2,1)} async-done(((bf16[2,1024,2048]{2,1,0:T(8,128)(2,1)}), bf16[2,1024,256]{2,1,0:T(8,128)(2,1)}) %reduce-scatter.5.cloned.1.call-update) | async-done | bytes 1048592 | tf_op jit(solution)/shard_map/reduce_scatter | solution.py:43
  323.8 3.3 copy.38
  327.1 10.0 %all-to-all-start.1 = ((bf16[2,1024,256]{2,0,1:T(2,128)(2,1)}), bf16[2,1024,256]{2,0,1:T(2,128)(2,1)S(1)}, u32[]{:S(2)}, u32[]{:S(2)}) async-start(bf16[2,1024,256]{2,0,1:T(2,128)(2,1)} %copy.38), calls=%async_computation.3 | async-start | bytes 2097152 | tf_op jit(solution)/shard_map/all_to_all | solution.py:46
  337.4 6.2 %scatter_custom_fusion.2 = f32[2048]{0:T(1024)S(1)} fusion(s32[1536]{0:T(1024)S(1)} %broadcast_select_fusion, f32[1536]{0:T(1024)S(1)} %reshape.147, f32[]{:T(128)} %constant.32.clone.1), kind=kCustom, calls=%fused_computation.40 | custom fusion | bytes 8196
  343.8 15.9 %reduce-scatter.3.cloned.1.call-done = bf16[256,256]{1,0:T(8,128)(2,1)} async-done(((bf16[256,2048]{1,0:T(8,128)(2,1)}), bf16[256,256]{1,0:T(8,128)(2,1)}) %reduce-scatter.3.cloned.1.call-update) | async-done | bytes 131088 | tf_op jit(solution)/shard_map/reduce_scatter | solution.py:52
  359.7 0.9 convert_element_type.44
  360.7 4.6 %all-to-all-done.1 = bf16[2,1024,256]{2,0,1:T(2,128)(2,1)S(1)} async-done(((bf16[2,1024,256]{2,0,1:T(2,128)(2,1)}), bf16[2,1024,256]{2,0,1:T(2,128)(2,1)S(1)}, u32[]{:S(2)}, u32[]{:S(2)}) %all-to-all-start.1) | async-done | bytes 1048608 | tf_op jit(solution)/shard_map/all_to_all | solution.py:46
  365.3 0.2 copy.39
  365.5 1.7 bitcast_multiply_fusion
  367.2 12.3 %scatter_fusion = f32[256,256]{1,0:T(8,128)S(1)} fusion(f32[256,256]{1,0:T(8,128)S(1)} %convert_element_type.44, s32[2048]{0:T(1024)S(1)} %bitcast.50, f32[2048,256]{1,0:T(8,128)} %bitcast_multiply_fusion), kind=kCustom, calls=%fused_computation.1 | custom fusion | flops 524288 | bytes 6299648 | tf_op jit(solution)/shard_map/scatter-add | solution.py:51
  379.5 0.7 convert_element_type.53
  (40 shorter events, 2.5 us)
Async XLA Ops:
  6.5 252.7 %copy-start = (bf16[2,176,2048]{2,1,0:T(8,128)(2,1)S(1)}, bf16[2,176,2048]{2,1,0:T(8,128)(2,1)}, u32[]{:S(2)}) copy-start(bf16[2,176,2048]{2,1,0:T(8,128)(2,1)} %param.14) | copy-start | bytes 4325380
  6.5 317.3 %reduce-scatter.5.cloned.1.call-start = ((), (), s32[]{:S(2)}) async-start(), calls=%async_computation.5 | async-start | bytes 9437184 | tf_op jit(solution)/shard_map/reduce_scatter | solution.py:43
  27.5 7.9 %copy-start.1 = (bf16[256,2048]{1,0:T(8,128)(2,1)S(1)}, bf16[256,2048]{1,0:T(8,128)(2,1)}, u32[]{:S(2)}) copy-start(bf16[256,2048]{1,0:T(8,128)(2,1)} %param.9) | copy-start | bytes 3145732
  27.8 0.7 copy-start.3
  27.8 0.8 copy-start.6
  27.8 0.9 copy-start.5
  243.4 8.4 %copy-start.2 = (bf16[2,2048,176]{1,2,0:T(8,128)(2,1)S(1)}, bf16[2,2048,176]{1,2,0:T(8,128)(2,1)}, u32[]{:S(2)}) copy-start(bf16[2,2048,176]{1,2,0:T(8,128)(2,1)} %param.12) | copy-start | bytes 4325380
  273.6 86.2 %reduce-scatter.3.cloned.1.call-start = ((), (), s32[]{:S(2)}) async-start(), calls=%async_computation.4 | async-start | bytes 1179648 | tf_op jit(solution)/shard_map/reduce_scatter | solution.py:52
  327.1 10.0 %copy-start.4 = (f32[256,6]{0,1:T(8,128)S(1)}, f32[256,6]{0,1:T(8,128)}, u32[]{:S(2)}) copy-start(f32[256,6]{0,1:T(8,128)} %param.11) | copy-start | bytes 18436
  327.1 38.2 %all-to-all-start.1 = ((bf16[2,1024,256]{2,0,1:T(2,128)(2,1)}), bf16[2,1024,256]{2,0,1:T(2,128)(2,1)S(1)}, u32[]{:S(2)}, u32[]{:S(2)}) async-start(bf16[2,1024,256]{2,0,1:T(2,128)(2,1)} %copy.38), calls=%async_computation.3 | async-start | bytes 2097152 | tf_op jit(solution)/shard_map/all_to_all | solution.py:46
Sparse Core Ops, SparseCore 0:
  273.7 50.0 reduce-scatter.4
  326.3 33.3 reduce-scatter.2
where the time goes:
time: 389 us; the launch traced here: 387 us
  blocking collectives  197 us (51%)
  waiting for transfers between devices  63.8 us (16%)
  local copies, waits for them, and re-layouts  38.9 us (10%)
  other arithmetic  35 us (9%)
  matrix products  28.5 us (7%)
  between operations  13.6 us (3%)
  starting transfers between devices  10.2 us (3%)
    all_to_all x1, blocking collectives, shards(): lax.all_to_all(outgoing, 'expert', split_axis=0, concat_axis=1, tiled=True)  197 us
    reduce_scatter x1, waiting for transfers between devices, shards(): lax.psum_scatter(widened.astype(jnp.bfloat16), 'seq', scatter_dimension=2...  43.2 us
    another operation x3, other arithmetic  18.4 us
    reduce_scatter x1, waiting for transfers between devices, shards(): lax.psum_scatter(shared_part.astype(jnp.bfloat16), 'seq', scatter_dimensi...  15.9 us
    dot_general x1, matrix products, shards(): jnp.einsum('erf,efd->erd', hidden, expert_down, preferred_element_type=jn...  14.3 us
    unnamed x20, local copies, waits for them, and re-layouts  14 us
    scatter-add x1, other arithmetic, shards(): jnp.zeros((rows, columns), jnp.float32).at[flat_slots].add(weighted)  12.3 us
    gather x1, local copies, waits for them, and re-layouts, shards(): outgoing = tokens[slot_tok.reshape(-1)].reshape(experts, capacity, width)  11 us
  transfers between devices with their start and end apart: 3, of which 3 were waited for; matrix products, arithmetic and copies ran while one was open for 5% of the time, Pallas kernels for 0%

commit v1 on v0

v1 whole, which is shorter than its diff:
```python
import functools
import jax
import jax.numpy as jnp
from jax import lax
from jax.experimental import pallas as pl
from jax.experimental.pallas import tpu as pltpu
from jax.sharding import PartitionSpec as P

MESH = pl.DeviceIdType.MESH
F32 = jnp.float32
BF16 = jnp.bfloat16
CAP = 32
NX = 4
NY = 4


def kernel(nz, ny, top, tokens, routes, gates, wg_h, wu_h, wd_h, sg_h, su_h, sd_h, out,
           wg, wu, wd, sg, su, sd, rank_m, gate_m, xout, arr, part, precv, total, thru, final,
           back, ret, acc,
           w_sem, l_sem, a_send, a_recv, x_send, xl_recv, xr_recv, h_send, hl_recv, hr_recv,
           c_send, c_recv, p_send, p_recv, f_send, fl_recv, fr_recv, g_send, gl_recv, gr_recv,
           r_send, r_recv):
    rows = tokens.shape[0]
    width = xout.shape[2]
    half = ny * CAP
    experts = xout.shape[0]
    block = 2 * half
    seq, exp = lax.axis_index("seq"), lax.axis_index("expert")
    x, c = seq // 2, seq % 2
    z, y = exp // ny, exp % ny
    right, left, across = (x + 1) % NX, (x + NX - 1) % NX, (x + 2) % NX
    to_right = (right * 2 + c, exp)
    to_left = (left * 2 + c, exp)
    to_core = (x * 2 + 1 - c, exp)

    def offset(k):
        step = (k + 1) // 2
        odd = k % 2
        return odd * step + (1 - odd) * ((nz - step) % nz)

    def remote(src, dst, send, recv, target):
        return pltpu.make_async_remote_copy(
            src_ref=src, dst_ref=dst, send_sem=send, recv_sem=recv,
            device_id=target, device_id_type=MESH)

    barrier = pltpu.get_barrier_semaphore()

    @pl.loop(1, nz * ny)
    def _(d):
        pl.semaphore_signal(barrier, inc=1, device_id=(seq, (exp + d) % (nz * ny)),
                            device_id_type=MESH)

    for target in (to_right, to_left, to_core):
        pl.semaphore_signal(barrier, inc=1, device_id=target, device_id_type=MESH)

    loads = [pltpu.make_async_copy(a, b, w_sem.at[i]) for i, (a, b) in enumerate(
        ((sg_h, sg), (su_h, su), (sd_h, sd), (wg_h, wg), (wu_h, wu), (wd_h, wd)))]
    for copy in loads:
        copy.start()

    eid = lax.broadcasted_iota(jnp.int32, (rows, experts), 1)
    chosen = jnp.zeros((rows, experts), F32)
    weight = jnp.zeros((rows, experts), F32)
    for k in range(top):
        hit = routes[:, k:k + 1] == eid
        chosen = chosen + jnp.where(hit, 1.0, 0.0)
        weight = weight + jnp.where(hit, gates[:, k:k + 1], 0.0)
    gate_m[...] = weight
    below = lax.broadcasted_iota(jnp.int32, (rows, rows), 0) > lax.broadcasted_iota(
        jnp.int32, (rows, rows), 1)
    rank = jnp.dot(jnp.where(below, 1.0, 0.0).astype(BF16), chosen.astype(BF16),
                   preferred_element_type=F32)
    rank_m[...] = jnp.where(chosen > 0.5, rank, -1.0).astype(BF16)

    pl.semaphore_wait(barrier, nz * ny - 1 + 3)

    def send_slots(k):
        zb = (z + offset(k)) % nz
        first = zb * (2 * ny)
        row = lax.broadcasted_iota(jnp.int32, (block, experts), 0)
        col = lax.broadcasted_iota(jnp.int32, (block, experts), 1)
        spread = jnp.where(row // CAP + first == col, 1.0, 0.0).astype(BF16)
        ranks = lax.dot_general(spread, rank_m[...], (((1,), (1,)), ((), ())),
                                preferred_element_type=F32)
        place = (lax.broadcasted_iota(jnp.int32, (block, rows), 0) % CAP).astype(F32)
        pick = jnp.where(ranks == place, 1.0, 0.0).astype(BF16)
        mine = tokens[:, pl.ds(pl.multiple_of(seq * width, width), width)]
        slots = jnp.dot(pick, mine, preferred_element_type=F32).astype(BF16)
        xout[pl.ds(first, 2 * ny)] = slots.reshape(2 * ny, CAP, width)
        for dy in range(ny):
            there = zb * ny + (y + dy) % ny
            src = xout.at[pl.ds(2 * there, 2)]
            dst = arr.at[x, c, k, :, dy * CAP:(dy + 1) * CAP, :]
            copy = remote(src, dst, a_send.at[k], a_recv.at[k], (seq, there))
            if dy:
                copy.start()
            else:
                @pl.when(k > 0)
                def _():
                    copy.start()

                @pl.when(k == 0)
                def _():
                    pltpu.make_async_copy(src, dst, l_sem.at[0]).start()

    def gather_neighbours(k):
        @pl.when(k == 0)
        def _():
            pltpu.make_async_copy(xout.at[0:2], arr.at[x, c, 0, :, 0:CAP, :], l_sem.at[0]).wait()
            rest = arr.at[x, c, 0, :, CAP:half, :]
            remote(rest, rest, a_send.at[0], a_recv.at[0], to_right).wait_recv()

        own = arr.at[x, c, k]

        @pl.when(k > 0)
        def _():
            remote(own, own, a_send.at[k], a_recv.at[k], to_right).wait_recv()

        remote(own, own, x_send.at[k], xl_recv.at[k], to_right).start()
        remote(own, own, x_send.at[k], xr_recv.at[k], to_left).start()
        remote(own, own, c_send.at[k], c_recv.at[k], to_core).start()

    def gather_across(k):
        from_left, from_right = arr.at[left, c, k], arr.at[right, c, k]
        remote(from_left, from_left, x_send.at[k], xl_recv.at[k], to_right).wait_recv()
        remote(from_left.at[0], from_left.at[0], h_send.at[k], hl_recv.at[k], to_right).start()
        remote(from_left, from_left, c_send.at[k], c_recv.at[k], to_core).start()
        remote(from_right, from_right, x_send.at[k], xr_recv.at[k], to_left).wait_recv()
        remote(from_right.at[1], from_right.at[1], h_send.at[k], hr_recv.at[k], to_left).start()
        remote(from_right, from_right, c_send.at[k], c_recv.at[k], to_core).start()

    def gather_core(k):
        far = arr.at[across, c, k]
        remote(far.at[0], far.at[0], h_send.at[k], hl_recv.at[k], to_right).wait_recv()
        remote(far.at[1], far.at[1], h_send.at[k], hr_recv.at[k], to_left).wait_recv()
        remote(far, far, c_send.at[k], c_recv.at[k], to_core).start()

    def send_part(j):
        remote(part.at[j], precv.at[j], p_send.at[j], p_recv.at[j], to_core).start()

    def down(hidden, weights):
        for parity, dst in ((1 - c, part), (c, total)):
            for xx in range(NX):
                cols = pl.ds(pl.multiple_of((2 * xx + parity) * width, width), width)
                value = jnp.dot(hidden, weights(cols), preferred_element_type=F32).astype(BF16)
                yield dst, xx, value

    def shared_part():
        for copy in loads[:3]:
            copy.wait()
        gate = jnp.dot(tokens[...], sg[...], preferred_element_type=F32)
        up = jnp.dot(tokens[...], su[...], preferred_element_type=F32)
        hidden = (gate / (1.0 + jnp.exp(-gate)) * up).astype(BF16)
        for dst, xx, value in down(hidden, lambda cols: sd[:, cols]):
            dst[0, xx] = value.reshape(2, half, width)
        send_part(0)

    def routed_part(k):
        @pl.when(k == 0)
        def _():
            for copy in loads[3:]:
                copy.wait()

        other = arr.at[:, 1 - c, k]
        remote(other, other, c_send.at[k], c_recv.at[k], to_core).wait_recv()
        for e in range(2):
            gate = jnp.zeros((half, wg.shape[2]), F32)
            up = jnp.zeros((half, wg.shape[2]), F32)
            for s in range(2 * NX):
                a = arr[s // 2, s % 2, k, e]
                gate = gate + jnp.dot(a, wg[e, s * width:(s + 1) * width],
                                      preferred_element_type=F32)
                up = up + jnp.dot(a, wu[e, s * width:(s + 1) * width],
                                  preferred_element_type=F32)
            hidden = (gate / (1.0 + jnp.exp(-gate)) * up).astype(BF16)
            for dst, xx, value in down(hidden, lambda cols: wd[e, :, cols]):
                dst[k + 1, xx, e] = value
        send_part(k + 1)

    def reduce_core(j):
        remote(part.at[j], precv.at[j], p_send.at[j], p_recv.at[j], to_core).wait_recv()

        def add(xx):
            total[j, xx] = (total[j, xx].astype(F32) + precv[j, xx].astype(F32)).astype(BF16)

        add(across)
        remote(total.at[j, across, 0], thru.at[0, j], f_send.at[j], fl_recv.at[j], to_right).start()
        remote(total.at[j, across, 1], thru.at[1, j], f_send.at[j], fr_recv.at[j], to_left).start()
        add(right)
        remote(total.at[j, right, 1], final.at[0, j, 1], g_send.at[j], gl_recv.at[j], to_right).start()
        add(left)
        remote(total.at[j, left, 0], final.at[1, j, 0], g_send.at[j], gr_recv.at[j], to_left).start()
        add(x)

    def reduce_across(j):
        remote(thru.at[0, j], thru.at[0, j], f_send.at[j], fl_recv.at[j], to_right).wait_recv()
        total[j, right, 0] = (total[j, right, 0].astype(F32) + thru[0, j].astype(F32)).astype(BF16)
        remote(total.at[j, right, 0], final.at[0, j, 0], g_send.at[j], gl_recv.at[j], to_right).start()
        remote(thru.at[1, j], thru.at[1, j], f_send.at[j], fr_recv.at[j], to_left).wait_recv()
        total[j, left, 1] = (total[j, left, 1].astype(F32) + thru[1, j].astype(F32)).astype(BF16)
        remote(total.at[j, left, 1], final.at[1, j, 1], g_send.at[j], gr_recv.at[j], to_left).start()

    def reduce_neighbours(j):
        remote(final.at[0, j], final.at[0, j], g_send.at[j], gl_recv.at[j], to_right).wait_recv()
        remote(final.at[1, j], final.at[1, j], g_send.at[j], gr_recv.at[j], to_left).wait_recv()
        value = total[j, x].astype(F32) + final[0, j].astype(F32) + final[1, j].astype(F32)

        @pl.when(j == 0)
        def _():
            acc[...] = value.reshape(rows, width)

        @pl.when(j > 0)
        def _():
            k = j - 1
            back[k] = value.astype(BF16)
            zb = (z + nz - offset(k)) % nz
            for dy in range(ny):
                there = zb * ny + (y + ny - dy) % ny
                src = back.at[k, :, dy * CAP:(dy + 1) * CAP, :]
                dst = ret.at[pl.ds(2 * exp, 2)]
                copy = remote(src, dst, r_send.at[k], r_recv.at[k], (seq, there))
                if dy:
                    copy.start()
                else:
                    @pl.when(k > 0)
                    def _():
                        copy.start()

                    @pl.when(k == 0)
                    def _():
                        pltpu.make_async_copy(src, dst, l_sem.at[1]).start()

    def combine(k):
        zb = (z + offset(k)) % nz
        first = zb * (2 * ny)

        @pl.when(k == 0)
        def _():
            pltpu.make_async_copy(ret.at[0:2], ret.at[0:2], l_sem.at[1]).wait()
            rest = ret.at[0:2 * ny - 2]
            remote(rest, rest, r_send.at[0], r_recv.at[0], to_right).wait_recv()

        @pl.when(k > 0)
        def _():
            rest = ret.at[0:2 * ny]
            remote(rest, rest, r_send.at[k], r_recv.at[k], to_right).wait_recv()

        row = lax.broadcasted_iota(jnp.int32, (experts, block), 0)
        col = lax.broadcasted_iota(jnp.int32, (experts, block), 1)
        spread = jnp.where(col // CAP + first == row, 1.0, 0.0).astype(BF16)
        ranks = jnp.dot(rank_m[...], spread, preferred_element_type=F32)
        place = (lax.broadcasted_iota(jnp.int32, (rows, block), 1) % CAP).astype(F32)
        here = ranks == place
        values = ret[pl.ds(first, 2 * ny)].reshape(block, width)
        left_over = gate_m[...]
        total_here = acc[...]
        for _ in range(2):
            piece = left_over.astype(BF16)
            left_over = left_over - piece.astype(F32)
            wide = jnp.dot(piece, spread, preferred_element_type=F32)
            mix = jnp.where(here, wide, 0.0).astype(BF16)
            total_here = total_here + jnp.dot(mix, values, preferred_element_type=F32)
        acc[...] = total_here

    def stage(body, index, count):
        @pl.when((index >= 0) & (index < count))
        def _():
            body(index)

    @pl.loop(0, nz + 7)
    def _(i):
        stage(send_slots, i, nz)
        stage(gather_neighbours, i - 1, nz)
        stage(gather_across, i - 2, nz)
        stage(gather_core, i - 3, nz)
        stage(reduce_neighbours, i - 5, nz + 1)
        stage(reduce_across, i - 4, nz + 1)
        stage(reduce_core, i - 3, nz + 1)

        @pl.when(i == 2)
        def _():
            shared_part()

        stage(routed_part, i - 3, nz)
        stage(combine, i - 7, nz)

    out[...] = acc[...].astype(out.dtype)

    @pl.loop(0, nz)
    def _(k):
        @pl.when(k == 0)
        def _():
            rest = xout.at[0:2 * ny - 2]
            remote(rest, rest, a_send.at[0], a_recv.at[0], to_right).wait_send()
            remote(rest, rest, r_send.at[0], r_recv.at[0], to_right).wait_send()

        @pl.when(k > 0)
        def _():
            rest = xout.at[0:2 * ny]
            remote(rest, rest, a_send.at[k], a_recv.at[k], to_right).wait_send()
            remote(rest, rest, r_send.at[k], r_recv.at[k], to_right).wait_send()

        two = arr.at[0:2, 0, k]
        remote(two, two, x_send.at[k], xl_recv.at[k], to_right).wait_send()
        one = arr.at[0, 0, k]
        remote(one, one, h_send.at[k], hl_recv.at[k], to_right).wait_send()
        four = arr.at[:, 0, k]
        remote(four, four, c_send.at[k], c_recv.at[k], to_core).wait_send()

    @pl.loop(0, nz + 1)
    def _(j):
        remote(part.at[j], precv.at[j], p_send.at[j], p_recv.at[j], to_core).wait_send()
        one = final.at[0, j]
        remote(one, one, f_send.at[j], fl_recv.at[j], to_right).wait_send()
        two = total.at[j, 0:2]
        remote(two, two, g_send.at[j], gl_recv.at[j], to_right).wait_send()


def layer(tokens, routes, gates, wg, wu, wd, sg, su, sd, nz):
    rows, width_all = tokens.shape
    width = width_all // (2 * NX)
    ny = lax.axis_size("expert") // nz
    experts = 2 * nz * ny
    half = ny * CAP
    assert rows == 2 * half
    dma = pltpu.SemaphoreType.DMA
    vm = pltpu.VMEM
    scratch = [vm(a.shape, BF16) for a in (wg, wu, wd, sg, su, sd)]
    scratch += [
        vm((rows, experts), BF16),
        vm((rows, experts), F32),
        vm((experts, CAP, width), BF16),
        vm((NX, 2, nz, 2, half, width), BF16),
        vm((nz + 1, NX, 2, half, width), BF16),
        vm((nz + 1, NX, 2, half, width), BF16),
        vm((nz + 1, NX, 2, half, width), BF16),
        vm((2, nz + 1, half, width), BF16),
        vm((2, nz + 1, 2, half, width), BF16),
        vm((nz, 2, half, width), BF16),
        vm((experts, CAP, width), BF16),
        vm((rows, width), F32),
    ]
    scratch += [dma((6,)), dma((2,))]
    scratch += [dma((nz,)) for _ in range(10)]
    scratch += [dma((nz + 1,)) for _ in range(8)]
    scratch += [dma((nz,)) for _ in range(2)]
    return pl.pallas_call(
        functools.partial(kernel, nz, ny, routes.shape[1]),
        out_shape=jax.ShapeDtypeStruct((rows, width), BF16),
        in_specs=[pl.BlockSpec(memory_space=pltpu.VMEM)] * 3
        + [pl.BlockSpec(memory_space=pl.ANY)] * 6,
        out_specs=pl.BlockSpec(memory_space=pltpu.VMEM),
        scratch_shapes=scratch,
        compiler_params=pltpu.CompilerParams(
            collective_id=0, has_side_effects=True, vmem_limit_bytes=60 * 1024 * 1024),
        cost_estimate=pl.CostEstimate(
            flops=7 * 10**9, bytes_accessed=12 * 10**6, transcendentals=10**6),
    )(tokens, routes, gates, wg, wu, wd, sg, su, sd)


def solution(mesh):
    nz = mesh.shape["expert"] // NY
    return jax.shard_map(
        functools.partial(layer, nz=nz),
        mesh=mesh,
        in_specs=(
            P("expert", None),
            P("expert", None),
            P("expert", None),
            P("expert", None, "seq"),
            P("expert", None, "seq"),
            P("expert", "seq", None),
            P(None, "seq"),
            P(None, "seq"),
            P("seq", None),
        ),
        out_specs=P("expert", "seq"),
        check_vma=False,
    )
```

time: 389 us -> 121 us (0.31)
  blocking collectives: 197 us -> 0 us
  Pallas kernels: 0 us -> 107 us
  waiting for transfers between devices: 63.8 us -> 0 us
  other arithmetic: 35 us -> 0 us
  matrix products: 28.5 us -> 0 us
  local copies, waits for them, and re-layouts: 38.9 us -> 13.6 us
  between operations: 13.6 us -> 0.02 us
  starting transfers between devices: 10.2 us -> 0 us
    all_to_all x1 -> x0, blocking collectives: 197 us -> none  [shards(): lax.all_to_all(outgoing, 'expert', split_axis=0, concat_axis=1, tiled=True)]
    pallas_call x0 -> x1, Pallas kernels: none -> 107 us  [layer(): pl.pallas_call(functools.partial(kernel, nz, ny, routes.shape[1]), out_sh...]
    reduce_scatter x2 -> x0, waiting for transfers between devices: 59.1 us -> none  [the longest x1 43.2 us: shards(): lax.psum_scatter(widened.astype(jnp.bfloat16), 'seq', scatter_dimension=2...]
    dot_general x4 -> x0, matrix products: 28.5 us -> none  [the longest x1 14.3 us: shards(): jnp.einsum('erf,efd->erd', hidden, expert_down, preferred_element_type=jn...]
    another operation x3 -> x0, other arithmetic: 18.4 us -> none
    scatter-add x1 -> x0, other arithmetic: 12.3 us -> none  [shards(): jnp.zeros((rows, columns), jnp.float32).at[flat_slots].add(weighted)]
    gather x1 -> x0, local copies, waits for them, and re-layouts: 11 us -> none  [shards(): outgoing = tokens[slot_tok.reshape(-1)].reshape(experts, capacity, width)]
    all_to_all x1 -> x0, starting transfers between devices: 9.99 us -> none  [shards(): lax.all_to_all(summed.astype(jnp.bfloat16), 'expert', split_axis=1, conca...]
  transfers between devices with their start and end apart: 3 -> 0, of which waited for: 3 -> 0; matrix products, arithmetic and copies ran while one was open for 5% -> 0% of each run, Pallas kernels for 0% -> 0%
where the time goes in v1:
time: 121 us; the launch traced here: 120 us
  Pallas kernels  107 us (88%)
  local copies, waits for them, and re-layouts  13.6 us (11%)
    pallas_call x1, Pallas kernels, layer(): pl.pallas_call(functools.partial(kernel, nz, ny, routes.shape[1]), out_sh...  107 us
    unnamed x13, local copies, waits for them, and re-layouts  13.6 us

profile of v1, /device:TPU:6, one launch (start us, length us, event | category | flops | bytes accessed | tf_op | source)
XLA Modules:
  0.0 120.4 jit_solution(12811367409582001479)
XLA Ops:
  0.0 1.5 %copy.10.routes = s32[256,6]{1,0:T(8,128)} copy(s32[256,6]{0,1:T(8,128)} %param.10) | data formatting | bytes 12288 | tf_op args[1]
  1.5 1.5 %copy.11.gates = f32[256,6]{1,0:T(8,128)} copy(f32[256,6]{0,1:T(8,128)} %param.11) | data formatting | bytes 12288 | tf_op args[2]
  3.0 0.0 copy-start.2
  3.0 2.7 %copy.14.sg_h = bf16[2048,352]{1,0:T(8,128)(2,1)} copy(bf16[2048,352]{0,1:T(8,128)(2,1)} %param.15) | data formatting | bytes 2883584 | tf_op args[6]
  5.7 0.0 copy-done.2
  5.7 0.0 copy-start
  5.7 1.6 %copy.15.su_h = bf16[2048,352]{1,0:T(8,128)(2,1)} copy(bf16[2048,352]{0,1:T(8,128)(2,1)S(1)} %copy-done.2) | data formatting | bytes 2883584 | tf_op args[7]
  7.3 0.0 copy-done
  7.3 0.0 copy-start.1
  7.3 2.4 %copy.12.wg_h = bf16[2,2048,176]{2,1,0:T(8,128)(2,1)} copy(bf16[2,2048,176]{1,2,0:T(8,128)(2,1)S(1)} %copy-done) | data formatting | bytes 2883584 | tf_op args[3]
  9.7 0.0 copy-done.1
  9.7 2.4 %copy.13.wu_h = bf16[2,2048,176]{2,1,0:T(8,128)(2,1)} copy(bf16[2,2048,176]{1,2,0:T(8,128)(2,1)S(1)} %copy-done.1) | data formatting | bytes 2883584 | tf_op args[4]
  12.1 106.8 %shard_map.91 = bf16[256,256]{1,0:T(8,128)(2,1)} custom-call(bf16[256,2048]{1,0:T(8,128)(2,1)} %tokens.1, s32[256,6]{1,0:T(8,128)} %copy.10.routes, f32[256,6]{1,0:T(8,128)} %copy.11.gates, bf16[2,2048,176]{2,1,0:T(8,128)(2,1)} %copy.12.wg_h, bf16[2,2048,176]{2,1,0:T(8,128)(2,1)} %copy.13.wu_h, bf16[2,176,2048]{2,1,0:T(8,128)(2,1)} %wd_h.1, ...), custom_call_target="tpu_custom_call" | custom-call | flops 7000000000 | bytes 12000000 | tf_op jit(solution)/shard_map/pallas_call | solution.py:347
  118.9 1.6 %copy.17 = bf16[256,256]{1,0:T(8,128)(2,1)} copy(bf16[256,256]{1,0:T(8,128)(2,1)} %shard_map.91) | data formatting | bytes 262144
Async XLA Ops:
  3.0 2.7 %copy-start.2 = (bf16[2048,352]{0,1:T(8,128)(2,1)S(1)}, bf16[2048,352]{0,1:T(8,128)(2,1)}, u32[]{:S(2)}) copy-start(bf16[2048,352]{0,1:T(8,128)(2,1)} %param.16) | copy-start | bytes 4325380
  5.7 1.6 %copy-start = (bf16[2,2048,176]{1,2,0:T(8,128)(2,1)S(1)}, bf16[2,2048,176]{1,2,0:T(8,128)(2,1)}, u32[]{:S(2)}) copy-start(bf16[2,2048,176]{1,2,0:T(8,128)(2,1)} %param.12) | copy-start | bytes 4325380
  7.3 2.4 %copy-start.1 = (bf16[2,2048,176]{1,2,0:T(8,128)(2,1)S(1)}, bf16[2,2048,176]{1,2,0:T(8,128)(2,1)}, u32[]{:S(2)}) copy-start(bf16[2,2048,176]{1,2,0:T(8,128)(2,1)} %param.13) | copy-start | bytes 4325380

commit v2 on v0

v2 whole, which is shorter than its diff:
```python
import functools
import jax
import jax.numpy as jnp
from jax import lax
from jax.experimental import pallas as pl
from jax.experimental.pallas import tpu as pltpu
from jax.sharding import PartitionSpec as P

MESH = pl.DeviceIdType.MESH
F32 = jnp.float32
BF16 = jnp.bfloat16
CAP = 32
NX = 4
NY = 4
PLAN = {8: ((4, -1, 0, 3, -3, 2, -2, 1), (0, 1), (0, -1))}
FLOW = (
    ("near", 1, 1, 1),
    ("sum1", 1, 1, 5),
    ("routed", 1, 1, 4),
    ("slots", 8, 1, 0),
    ("mix", 3, 2, 11),
    ("far", 1, 1, 2),
    ("core", 1, 1, 3),
    ("shared", 1, 1, 0),
    ("sum3", 1, 1, 6),
    ("sum2", 1, 1, 5),
)


def plan_of(nz):
    default = [0] + [d for k in range(1, nz) for d in (k, -k)][:nz - 1]
    plan = PLAN.get(nz, (tuple(default), (0, 1), (0, -1)))
    return [[d % nz for d in part] for part in plan]


def dot_nt(a, b):
    return lax.dot_general(a, b, (((1,), (1,)), ((), ())), preferred_element_type=F32)


def kernel(nz, ny, top, tokens, routes, gates, wg_h, wu_h, wd_h, sg_h, su_h, sd_h, out,
           wg, wu, wd, sg, su, sd, rank_t, rank_m, gate_m, xout, xwide, arr, part, precv, total, thru, final,
           back, ret, rwide, twide, acc,
           w_sem, l_sem, a_send, a_recv, x_send, xl_recv, xr_recv, h_send, hl_recv, hr_recv,
           c_send, c_recv, p_send, p_recv, f_send, fl_recv, fr_recv, g_send, gl_recv, gr_recv,
           r_send, r_recv):
    rows = tokens.shape[0]
    width = xout.shape[2]
    half = ny * CAP
    experts = xout.shape[0]
    block = 2 * half
    seq, exp = lax.axis_index("seq"), lax.axis_index("expert")
    x, c = seq // 2, seq % 2
    z, y = exp // ny, exp % ny
    right, left, across = (x + 1) % NX, (x + NX - 1) % NX, (x + 2) % NX
    to_right = (right * 2 + c, exp)
    to_left = (left * 2 + c, exp)
    to_core = (x * 2 + 1 - c, exp)

    order, *whole = plan_of(nz)
    zero = order.index(0)
    wide_out, wide_in = [sorted(order.index(d) for d in part) for part in whole]

    def offset(p):
        value = 0
        for q, d in enumerate(order):
            value = jnp.where(p == q, d, value)
        return value

    def within(p, some):
        hit = p == nz + 1
        for q in some:
            hit = hit | (p == q)
        return hit

    def remote(src, dst, send, recv, target):
        return pltpu.make_async_remote_copy(
            src_ref=src, dst_ref=dst, send_sem=send, recv_sem=recv,
            device_id=target, device_id_type=MESH)

    barrier = pltpu.get_barrier_semaphore()

    @pl.loop(1, nz * ny)
    def _(d):
        pl.semaphore_signal(barrier, inc=1, device_id=(seq, (exp + d) % (nz * ny)),
                            device_id_type=MESH)

    for target in (to_right, to_left, to_core):
        pl.semaphore_signal(barrier, inc=1, device_id=target, device_id_type=MESH)

    loads = [pltpu.make_async_copy(a, b, w_sem.at[i]) for i, (a, b) in enumerate(
        ((sg_h, sg), (su_h, su), (sd_h, sd), (wg_h, wg), (wu_h, wu), (wd_h, wd)))]
    for copy in loads:
        copy.start()

    eid = lax.broadcasted_iota(jnp.int32, (experts, rows), 0)
    chosen = jnp.zeros((experts, rows), F32)
    for k in range(top):
        chosen = chosen + jnp.where(routes[k:k + 1, :] == eid, 1.0, 0.0)
    row = lax.broadcasted_iota(jnp.int32, (rows, rows), 0)
    col = lax.broadcasted_iota(jnp.int32, (rows, rows), 1)
    before = jnp.where(row < col, 1.0, 0.0).astype(BF16)
    rank = jnp.dot(chosen.astype(BF16), before, preferred_element_type=F32)
    rank_t[...] = jnp.where(chosen > 0.5, rank, -1.0).astype(BF16)

    pl.semaphore_wait(barrier, nz * ny - 1 + 3)

    def send_one(src, dst, p, dy, send, recv, target, local):
        copy = remote(src, dst, send.at[p], recv.at[p], target)
        if dy:
            copy.start()
        else:
            @pl.when(p != zero)
            def _():
                copy.start()

            @pl.when(p == zero)
            def _():
                pltpu.make_async_copy(src, dst, l_sem.at[local]).start()

    def slots_stage(p):
        zb = (z + offset(p)) % nz
        first = zb * (2 * ny)
        row = lax.broadcasted_iota(jnp.int32, (block, experts), 0)
        col = lax.broadcasted_iota(jnp.int32, (block, experts), 1)
        spread = jnp.where(row // CAP + first == col, 1.0, 0.0).astype(BF16)
        ranks = jnp.dot(spread, rank_t[...], preferred_element_type=F32)
        place = (lax.broadcasted_iota(jnp.int32, (block, rows), 0) % CAP).astype(F32)
        pick = jnp.where(ranks == place, 1.0, 0.0).astype(BF16)

        def gathered(s):
            mine = tokens[:, pl.ds(pl.multiple_of(s * width, width), width)]
            slots = jnp.dot(pick, mine, preferred_element_type=F32).astype(BF16)
            return slots.reshape(2 * ny, CAP, width)

        @pl.when(jnp.logical_not(within(p, wide_out)))
        def _():
            xout[pl.ds(first, 2 * ny)] = gathered(seq)
            for dy in range(ny):
                there = zb * ny + (y + dy) % ny
                send_one(xout.at[pl.ds(2 * there, 2)],
                         arr.at[x, c, p, :, dy * CAP:(dy + 1) * CAP, :],
                         p, dy, a_send, a_recv, (seq, there), 0)

        for f, q in enumerate(wide_out):
            @pl.when(p == q)
            def _():
                for xx in range(NX):
                    xwide[f, xx] = gathered(2 * xx + c)
                for dy in range(ny):
                    yy = (y + dy) % ny
                    send_one(xwide.at[f, :, pl.ds(2 * yy, 2)],
                             arr.at[:, c, p, :, dy * CAP:(dy + 1) * CAP, :],
                             p, dy, a_send, a_recv, (seq, zb * ny + yy), 0)

    def arrived(p, all_of, rest_of, recv, local):
        @pl.when(p != zero)
        def _():
            remote(all_of, all_of, a_send.at[p], recv.at[p], to_right).wait_recv()

        @pl.when(p == zero)
        def _():
            first = all_of.at[(slice(None),) * (len(all_of.shape) - 3)
                              + ((slice(None), slice(0, CAP)) if local == 0 else (slice(0, 2),))]
            pltpu.make_async_copy(first, first, l_sem.at[local]).wait()
            remote(rest_of, rest_of, a_send.at[p], recv.at[p], to_right).wait_recv()

    def near_stage(p):
        @pl.when(within(p, wide_out))
        def _():
            own = arr.at[:, c, p]
            arrived(p, own, arr.at[:, c, p, :, CAP:half, :], a_recv, 0)
            remote(own, own, c_send.at[p], c_recv.at[p], to_core).start()

        @pl.when(jnp.logical_not(within(p, wide_out)))
        def _():
            own = arr.at[x, c, p]
            arrived(p, own, arr.at[x, c, p, :, CAP:half, :], a_recv, 0)
            remote(own, own, x_send.at[p], xl_recv.at[p], to_right).start()
            remote(own, own, x_send.at[p], xr_recv.at[p], to_left).start()
            remote(own, own, c_send.at[p], c_recv.at[p], to_core).start()

    def far_stage(p):
        @pl.when(jnp.logical_not(within(p, wide_out)))
        def _():
            from_left, from_right = arr.at[left, c, p], arr.at[right, c, p]
            remote(from_left, from_left, x_send.at[p], xl_recv.at[p], to_right).wait_recv()
            remote(from_left.at[0], from_left.at[0], h_send.at[p], hl_recv.at[p], to_right).start()
            remote(from_left, from_left, c_send.at[p], c_recv.at[p], to_core).start()
            remote(from_right, from_right, x_send.at[p], xr_recv.at[p], to_left).wait_recv()
            remote(from_right.at[1], from_right.at[1], h_send.at[p], hr_recv.at[p], to_left).start()
            remote(from_right, from_right, c_send.at[p], c_recv.at[p], to_core).start()

    def core_stage(p):
        @pl.when(jnp.logical_not(within(p, wide_out)))
        def _():
            far = arr.at[across, c, p]
            remote(far.at[0], far.at[0], h_send.at[p], hl_recv.at[p], to_right).wait_recv()
            remote(far.at[1], far.at[1], h_send.at[p], hr_recv.at[p], to_left).wait_recv()
            remote(far, far, c_send.at[p], c_recv.at[p], to_core).start()

    def send_part(j):
        remote(part.at[j], precv.at[j], p_send.at[j], p_recv.at[j], to_core).start()

    def down(hidden, weights):
        for parity, dst in ((1 - c, part), (c, total)):
            for xx in range(NX):
                cols = pl.ds(pl.multiple_of((2 * xx + parity) * width, width), width)
                value = jnp.dot(hidden, weights(cols), preferred_element_type=F32).astype(BF16)
                yield dst, xx, value

    def turn_tables():
        eid = lax.broadcasted_iota(jnp.int32, (experts, rows), 0)
        weight = jnp.zeros((experts, rows), F32)
        for k in range(top):
            weight = weight + jnp.where(routes[k:k + 1, :] == eid, gates[k:k + 1, :], 0.0)
        row = lax.broadcasted_iota(jnp.int32, (rows, rows), 0)
        col = lax.broadcasted_iota(jnp.int32, (rows, rows), 1)
        same = jnp.where(row == col, 1.0, 0.0).astype(BF16)
        high = weight.astype(BF16)
        low = (weight - high.astype(F32)).astype(BF16)
        rank_m[...] = dot_nt(same, rank_t[...]).astype(BF16)
        gate_m[0] = dot_nt(same, high).astype(BF16)
        gate_m[1] = dot_nt(same, low).astype(BF16)

    def shared_stage(_):
        turn_tables()
        for copy in loads[:3]:
            copy.wait()
        gate = dot_nt(tokens[...], sg[...])
        up = dot_nt(tokens[...], su[...])
        hidden = (gate / (1.0 + jnp.exp(-gate)) * up).astype(BF16)
        for dst, xx, value in down(hidden, lambda cols: sd[:, cols]):
            dst[nz, xx] = value.reshape(2, half, width)
        send_part(nz)

    def routed_stage(p):
        @pl.when(p == 0)
        def _():
            for copy in loads[3:]:
                copy.wait()

        other = arr.at[:, 1 - c, p]
        remote(other, other, c_send.at[p], c_recv.at[p], to_core).wait_recv()
        for e in range(2):
            gate = jnp.zeros((half, wg.shape[1]), F32)
            up = jnp.zeros((half, wg.shape[1]), F32)
            for s in range(2 * NX):
                a = arr[s // 2, s % 2, p, e]
                gate = gate + dot_nt(a, wg[e, :, s * width:(s + 1) * width])
                up = up + dot_nt(a, wu[e, :, s * width:(s + 1) * width])
            hidden = (gate / (1.0 + jnp.exp(-gate)) * up).astype(BF16)
            for dst, xx, value in down(hidden, lambda cols: wd[e, :, cols]):
                dst[p, xx, e] = value
        send_part(p)

    def sum1_stage(j):
        remote(part.at[j], precv.at[j], p_send.at[j], p_recv.at[j], to_core).wait_recv()

        def add(xx):
            value = total[j, xx].astype(F32) + precv[j, xx].astype(F32)
            if not wide_in:
                total[j, xx] = value.astype(BF16)
                return

            @pl.when(j < nz)
            def _():
                total[j, xx] = value.astype(BF16)

            @pl.when(j == nz)
            def _():
                total[j, xx] = (value + twide[xx].reshape(2, half, width)).astype(BF16)

        @pl.when(jnp.logical_not(within(j, wide_in)))
        def _():
            add(across)
            remote(total.at[j, across, 0], thru.at[0, j], f_send.at[j], fl_recv.at[j], to_right).start()
            remote(total.at[j, across, 1], thru.at[1, j], f_send.at[j], fr_recv.at[j], to_left).start()
            add(right)
            remote(total.at[j, right, 1], final.at[0, j, 1], g_send.at[j], gl_recv.at[j], to_right).start()
            add(left)
            remote(total.at[j, left, 0], final.at[1, j, 0], g_send.at[j], gr_recv.at[j], to_left).start()
            add(x)

        for f, q in enumerate(wide_in):
            @pl.when(j == q)
            def _():
                for xx in range(NX):
                    total[q, xx] = (total[q, xx].astype(F32) + precv[q, xx].astype(F32)).astype(BF16)
                zb = (z + nz - order[q]) % nz
                for dy in range(ny):
                    there = zb * ny + (y + ny - dy) % ny
                    send_one(total.at[q, :, :, dy * CAP:(dy + 1) * CAP, :],
                             rwide.at[f, :, pl.ds(2 * y, 2)],
                             j, dy, r_send, r_recv, (seq, there), 1)

    def sum2_stage(j):
        @pl.when(jnp.logical_not(within(j, wide_in)))
        def _():
            remote(thru.at[0, j], thru.at[0, j], f_send.at[j], fl_recv.at[j], to_right).wait_recv()
            total[j, right, 0] = (total[j, right, 0].astype(F32) + thru[0, j].astype(F32)).astype(BF16)
            remote(total.at[j, right, 0], final.at[0, j, 0], g_send.at[j], gl_recv.at[j], to_right).start()
            remote(thru.at[1, j], thru.at[1, j], f_send.at[j], fr_recv.at[j], to_left).wait_recv()
            total[j, left, 1] = (total[j, left, 1].astype(F32) + thru[1, j].astype(F32)).astype(BF16)
            remote(total.at[j, left, 1], final.at[1, j, 1], g_send.at[j], gr_recv.at[j], to_left).start()

    def sum3_stage(j):
        @pl.when(jnp.logical_not(within(j, wide_in)))
        def _():
            remote(final.at[0, j], final.at[0, j], g_send.at[j], gl_recv.at[j], to_right).wait_recv()
            remote(final.at[1, j], final.at[1, j], g_send.at[j], gr_recv.at[j], to_left).wait_recv()
            value = total[j, x].astype(F32) + final[0, j].astype(F32) + final[1, j].astype(F32)

            @pl.when(j == nz)
            def _():
                acc[...] = acc[...] + value.reshape(rows, width)

            @pl.when(j < nz)
            def _():
                back[j] = value.astype(BF16)
                zb = (z + nz - offset(j)) % nz
                for dy in range(ny):
                    there = zb * ny + (y + ny - dy) % ny
                    send_one(back.at[j, :, dy * CAP:(dy + 1) * CAP, :], ret.at[pl.ds(2 * exp, 2)],
                             j, dy, r_send, r_recv, (seq, there), 1)

    def mix_stage(p):
        zb = (z + offset(p)) % nz
        first = zb * (2 * ny)

        row = lax.broadcasted_iota(jnp.int32, (experts, block), 0)
        col = lax.broadcasted_iota(jnp.int32, (experts, block), 1)
        spread = jnp.where(col // CAP + first == row, 1.0, 0.0).astype(BF16)
        ranks = jnp.dot(rank_m[...], spread, preferred_element_type=F32)
        place = (lax.broadcasted_iota(jnp.int32, (rows, block), 1) % CAP).astype(F32)
        here = ranks == place
        pieces = [jnp.where(here, jnp.dot(gate_m[piece], spread, preferred_element_type=F32),
                            0.0).astype(BF16) for piece in range(2)]

        def mixed(values):
            values = values.reshape(block, width)
            return sum(jnp.dot(piece, values, preferred_element_type=F32) for piece in pieces)

        @pl.when(jnp.logical_not(within(p, wide_in)))
        def _():
            arrived(p, ret.at[0:2 * ny], ret.at[0:2 * ny - 2], r_recv, 1)
            acc[...] = acc[...] + mixed(ret[pl.ds(first, 2 * ny)])

        for f, q in enumerate(wide_in):
            @pl.when(p == q)
            def _():
                arrived(p, rwide.at[f], rwide.at[f, :, 0:2 * ny - 2], r_recv, 1)
                for xx in range(NX):
                    if f == 0:
                        twide[xx] = mixed(rwide[f, xx])
                    else:
                        twide[xx] = twide[xx] + mixed(rwide[f, xx])

    stages = {
        "slots": (slots_stage, nz), "near": (near_stage, nz), "far": (far_stage, nz),
        "core": (core_stage, nz), "shared": (shared_stage, 1), "routed": (routed_stage, nz),
        "sum1": (sum1_stage, nz + 1), "sum2": (sum2_stage, nz + 1), "sum3": (sum3_stage, nz + 1),
        "mix": (mix_stage, nz),
    }
    last = max(first + -(-stages[name][1] * den // num) for name, num, den, first in FLOW)
    acc[...] = jnp.zeros_like(acc)

    @pl.loop(0, last)
    def _(i):
        for name, num, den, first in FLOW:
            body, count = stages[name]

            def reached(steps):
                return jnp.minimum(num * jnp.maximum(steps, 0) // den, count)

            pl.loop(reached(i - first), reached(i + 1 - first))(body)

    out[...] = acc[...].astype(out.dtype)

    for p in range(nz):
        skip = 2 if p == zero else 0

        def sent(narrow, some, broad):
            if p in some:
                return broad.at[some.index(p), :, 0:2 * ny - skip]
            return narrow.at[0:2 * ny - skip]

        out_part, in_part = sent(xout, wide_out, xwide), sent(ret, wide_in, rwide)
        remote(out_part, out_part, a_send.at[p], a_recv.at[p], to_right).wait_send()
        remote(in_part, in_part, r_send.at[p], r_recv.at[p], to_right).wait_send()
        four = arr.at[:, 0, p]
        remote(four, four, c_send.at[p], c_recv.at[p], to_core).wait_send()
        if p not in wide_out:
            two, one = arr.at[0:2, 0, p], arr.at[0, 0, p]
            remote(two, two, x_send.at[p], xl_recv.at[p], to_right).wait_send()
            remote(one, one, h_send.at[p], hl_recv.at[p], to_right).wait_send()
    for j in range(nz + 1):
        remote(part.at[j], precv.at[j], p_send.at[j], p_recv.at[j], to_core).wait_send()
        if j not in wide_in:
            one, two = final.at[0, j], total.at[j, 0:2]
            remote(one, one, f_send.at[j], fl_recv.at[j], to_right).wait_send()
            remote(two, two, g_send.at[j], gl_recv.at[j], to_right).wait_send()


def layer(tokens, routes, gates, wg, wu, wd, sg, su, sd, nz):
    rows, width_all = tokens.shape
    routes, gates, sg, su = routes.T, gates.T, sg.T, su.T
    wg, wu = wg.transpose(0, 2, 1), wu.transpose(0, 2, 1)
    width = width_all // (2 * NX)
    ny = lax.axis_size("expert") // nz
    experts = 2 * nz * ny
    half = ny * CAP
    out_wide, in_wide = [max(len(part), 1) for part in plan_of(nz)[1:]]
    assert rows == 2 * half
    dma = pltpu.SemaphoreType.DMA
    vm = pltpu.VMEM
    scratch = [vm(a.shape, BF16) for a in (wg, wu, wd, sg, su, sd)]
    scratch += [
        vm((experts, rows), BF16),
        vm((rows, experts), BF16),
        vm((2, rows, experts), BF16),
        vm((experts, CAP, width), BF16),
        vm((out_wide, NX, 2 * ny, CAP, width), BF16),
        vm((NX, 2, nz, 2, half, width), BF16),
        vm((nz + 1, NX, 2, half, width), BF16),
        vm((nz + 1, NX, 2, half, width), BF16),
        vm((nz + 1, NX, 2, half, width), BF16),
        vm((2, nz + 1, half, width), BF16),
        vm((2, nz + 1, 2, half, width), BF16),
        vm((nz, 2, half, width), BF16),
        vm((experts, CAP, width), BF16),
        vm((in_wide, NX, 2 * ny, CAP, width), BF16),
        vm((NX, rows, width), F32),
        vm((rows, width), F32),
    ]
    scratch += [dma((6,)), dma((2,))]
    scratch += [dma((nz,)) for _ in range(10)]
    scratch += [dma((nz + 1,)) for _ in range(8)]
    scratch += [dma((nz,)) for _ in range(2)]
    return pl.pallas_call(
        functools.partial(kernel, nz, ny, routes.shape[0]),
        out_shape=jax.ShapeDtypeStruct((rows, width), BF16),
        in_specs=[pl.BlockSpec(memory_space=pltpu.VMEM)] * 3
        + [pl.BlockSpec(memory_space=pl.ANY)] * 6,
        out_specs=pl.BlockSpec(memory_space=pltpu.VMEM),
        scratch_shapes=scratch,
        compiler_params=pltpu.CompilerParams(
            collective_id=0, has_side_effects=True, vmem_limit_bytes=60 * 1024 * 1024),
        cost_estimate=pl.CostEstimate(
            flops=7 * 10**9, bytes_accessed=12 * 10**6, transcendentals=10**6),
    )(tokens, routes, gates, wg, wu, wd, sg, su, sd)


def solution(mesh):
    nz = mesh.shape["expert"] // NY
    return jax.shard_map(
        functools.partial(layer, nz=nz),
        mesh=mesh,
        in_specs=(
            P("expert", None),
            P("expert", None),
            P("expert", None),
            P("expert", None, "seq"),
            P("expert", None, "seq"),
            P("expert", "seq", None),
            P(None, "seq"),
            P(None, "seq"),
            P("seq", None),
        ),
        out_specs=P("expert", "seq"),
        check_vma=False,
    )
```

time: 389 us -> 90.6 us (0.23)
  the two profiles are of different devices: /device:TPU:6 before, /device:TPU:32 now
where the time goes in v2:
time: 90.6 us; the launch traced here: 90.5 us
  Pallas kernels  88.9 us (98%)
  local copies, waits for them, and re-layouts  1.57 us (2%)
    pallas_call x1, Pallas kernels, layer(): pl.pallas_call(functools.partial(kernel, nz, ny, routes.shape[0]), out_sh...  88.9 us

profile of v2, /device:TPU:32, one launch (start us, length us, event | category | flops | bytes accessed | tf_op | source)
XLA Modules:
  0.0 90.5 jit_solution(2457129747097746836)
XLA Ops:
  0.0 88.9 %shard_map.91 = bf16[256,256]{1,0:T(8,128)(2,1)} custom-call(bf16[256,2048]{1,0:T(8,128)(2,1)} %tokens.1, s32[6,256]{1,0:T(8,128)} %bitcast.10, f32[6,256]{1,0:T(8,128)} %bitcast.11, bf16[2,176,2048]{2,1,0:T(8,128)(2,1)} %bitcast.6, bf16[2,176,2048]{2,1,0:T(8,128)(2,1)} %bitcast.7, bf16[2,176,2048]{2,1,0:T(8,128)(2,1)} %wd_h.1, bf16[352,2048]{1,0:T(8,128)(2,1)} %bitcast.8, ...), custom_call_target="tpu_custom_call" | custom-call | flops 7000000000 | bytes 12000000 | tf_op jit(solution)/shard_map/pallas_call | solution.py:439
  88.9 1.6 %copy.11 = bf16[256,256]{1,0:T(8,128)(2,1)} copy(bf16[256,256]{1,0:T(8,128)(2,1)} %shard_map.91) | data formatting | bytes 262144

commit v3 on v2

--- a/solution.py
+++ b/solution.py
@@ -12,6 +12,7 @@
 CAP = 32
 NX = 4
 NY = 4
+EARLY = 8
 PLAN = {8: ((4, -1, 0, 3, -3, 2, -2, 1), (0, 1), (0, -1))}
 FLOW = (
     ("near", 1, 1, 1),
@@ -37,8 +38,8 @@
     return lax.dot_general(a, b, (((1,), (1,)), ((), ())), preferred_element_type=F32)
 
 
-def kernel(nz, ny, top, tokens, routes, gates, wg_h, wu_h, wd_h, sg_h, su_h, sd_h, out,
-           wg, wu, wd, sg, su, sd, rank_t, rank_m, gate_m, xout, xwide, arr, part, precv, total, thru, final,
+def kernel(nz, ny, top, tokens_h, routes_h, gates_h, wg_h, wu_h, wd_h, sg_h, su_h, sd_h, out,
+           tokens, routes, gates, wg, wu, wd, sg, su, sd, rank_t, rank_m, gate_m, xout, xwide, arr, part, precv, total, thru, final,
            back, ret, rwide, twide, acc,
            w_sem, l_sem, a_send, a_recv, x_send, xl_recv, xr_recv, h_send, hl_recv, hr_recv,
            c_send, c_recv, p_send, p_recv, f_send, fl_recv, fr_recv, g_send, gl_recv, gr_recv,
@@ -77,6 +78,11 @@
             src_ref=src, dst_ref=dst, send_sem=send, recv_sem=recv,
             device_id=target, device_id_type=MESH)
 
+    small = [pltpu.make_async_copy(a, b, w_sem.at[6 + i]) for i, (a, b) in enumerate(
+        ((routes_h, routes), (tokens_h, tokens), (gates_h, gates)))]
+    for copy in small:
+        copy.start()
+
     barrier = pltpu.get_barrier_semaphore()
 
     @pl.loop(1, nz * ny)
@@ -89,8 +95,7 @@
 
     loads = [pltpu.make_async_copy(a, b, w_sem.at[i]) for i, (a, b) in enumerate(
         ((sg_h, sg), (su_h, su), (sd_h, sd), (wg_h, wg), (wu_h, wu), (wd_h, wd)))]
-    for copy in loads:
-        copy.start()
+    small[0].wait()
 
     eid = lax.broadcasted_iota(jnp.int32, (experts, rows), 0)
     chosen = jnp.zeros((experts, rows), F32)
@@ -102,8 +107,6 @@
     rank = jnp.dot(chosen.astype(BF16), before, preferred_element_type=F32)
     rank_t[...] = jnp.where(chosen > 0.5, rank, -1.0).astype(BF16)
 
-    pl.semaphore_wait(barrier, nz * ny - 1 + 3)
-
     def send_one(src, dst, p, dy, send, recv, target, local):
         copy = remote(src, dst, send.at[p], recv.at[p], target)
         if dy:
@@ -117,7 +120,7 @@
             def _():
                 pltpu.make_async_copy(src, dst, l_sem.at[local]).start()
 
-    def slots_stage(p):
+    def fill_slots(p):
         zb = (z + offset(p)) % nz
         first = zb * (2 * ny)
         row = lax.broadcasted_iota(jnp.int32, (block, experts), 0)
@@ -135,6 +138,22 @@
         @pl.when(jnp.logical_not(within(p, wide_out)))
         def _():
             xout[pl.ds(first, 2 * ny)] = gathered(seq)
+
+        for f, q in enumerate(wide_out):
+            @pl.when(p == q)
+            def _():
+                for xx in range(NX):
+                    xwide[f, xx] = gathered(2 * xx + c)
+
+    def slots_stage(p):
+        zb = (z + offset(p)) % nz
+
+        @pl.when(p >= EARLY)
+        def _():
+            fill_slots(p)
+
+        @pl.when(jnp.logical_not(within(p, wide_out)))
+        def _():
             for dy in range(ny):
                 there = zb * ny + (y + dy) % ny
                 send_one(xout.at[pl.ds(2 * there, 2)],
@@ -144,13 +163,17 @@
         for f, q in enumerate(wide_out):
             @pl.when(p == q)
             def _():
-                for xx in range(NX):
-                    xwide[f, xx] = gathered(2 * xx + c)
                 for dy in range(ny):
                     yy = (y + dy) % ny
                     send_one(xwide.at[f, :, pl.ds(2 * yy, 2)],
                              arr.at[:, c, p, :, dy * CAP:(dy + 1) * CAP, :],
                              p, dy, a_send, a_recv, (seq, zb * ny + yy), 0)
+
+    small[1].wait()
+    for copy in loads:
+        copy.start()
+    pl.loop(0, min(EARLY, nz))(fill_slots)
+    pl.semaphore_wait(barrier, nz * ny - 1 + 3)
 
     def arrived(p, all_of, rest_of, recv, local):
         @pl.when(p != zero)
@@ -209,6 +232,7 @@
                 yield dst, xx, value
 
     def turn_tables():
+        small[2].wait()
         eid = lax.broadcasted_iota(jnp.int32, (experts, rows), 0)
         weight = jnp.zeros((experts, rows), F32)
         for k in range(top):
@@ -413,7 +437,7 @@
     assert rows == 2 * half
     dma = pltpu.SemaphoreType.DMA
     vm = pltpu.VMEM
-    scratch = [vm(a.shape, BF16) for a in (wg, wu, wd, sg, su, sd)]
+    scratch = [vm(a.shape, a.dtype) for a in (tokens, routes, gates, wg, wu, wd, sg, su, sd)]
     scratch += [
         vm((experts, rows), BF16),
         vm((rows, experts), BF16),
@@ -432,15 +456,14 @@
         vm((NX, rows, width), F32),
         vm((rows, width), F32),
     ]
-    scratch += [dma((6,)), dma((2,))]
+    scratch += [dma((9,)), dma((2,))]
     scratch += [dma((nz,)) for _ in range(10)]
     scratch += [dma((nz + 1,)) for _ in range(8)]
     scratch += [dma((nz,)) for _ in range(2)]
     return pl.pallas_call(
         functools.partial(kernel, nz, ny, routes.shape[0]),
         out_shape=jax.ShapeDtypeStruct((rows, width), BF16),
-        in_specs=[pl.BlockSpec(memory_space=pltpu.VMEM)] * 3
-        + [pl.BlockSpec(memory_space=pl.ANY)] * 6,
+        in_specs=[pl.BlockSpec(memory_space=pl.ANY)] * 9,
         out_specs=pl.BlockSpec(memory_space=pltpu.VMEM),
         scratch_shapes=scratch,
         compiler_params=pltpu.CompilerParams(

time: 90.6 us -> 88.8 us (0.980)
  the two profiles are of different devices: /device:TPU:32 before, /device:TPU:6 now
where the time goes in v3:
time: 88.8 us; the launch traced here: 87.8 us
  Pallas kernels  86.2 us (97%)
  local copies, waits for them, and re-layouts  1.57 us (2%)
    pallas_call x1, Pallas kernels, layer(): pl.pallas_call(functools.partial(kernel, nz, ny, routes.shape[0]), out_sh...  86.2 us

profile of v3, /device:TPU:6, one launch (start us, length us, event | category | flops | bytes accessed | tf_op | source)
XLA Modules:
  0.0 87.8 jit_solution(16784993515473192078)
XLA Ops:
  0.0 86.2 %shard_map.91 = bf16[256,256]{1,0:T(8,128)(2,1)} custom-call(bf16[256,2048]{1,0:T(8,128)(2,1)} %tokens_h.1, s32[6,256]{1,0:T(8,128)} %bitcast.10, f32[6,256]{1,0:T(8,128)} %bitcast.11, bf16[2,176,2048]{2,1,0:T(8,128)(2,1)} %bitcast.6, bf16[2,176,2048]{2,1,0:T(8,128)(2,1)} %bitcast.7, bf16[2,176,2048]{2,1,0:T(8,128)(2,1)} %wd_h.1, bf16[352,2048]{1,0:T(8,128)(2,1)} %bitcast.8, ...), custom_call_target="tpu_custom_call" | custom-call | flops 7000000000 | bytes 12000000 | tf_op jit(solution)/shard_map/pallas_call | solution.py:463
  86.2 1.6 %copy.11 = bf16[256,256]{1,0:T(8,128)(2,1)} copy(bf16[256,256]{1,0:T(8,128)(2,1)} %shard_map.91) | data formatting | bytes 262144

commit v4 on v3

--- a/solution.py
+++ b/solution.py
@@ -13,18 +13,18 @@
 NX = 4
 NY = 4
 EARLY = 8
-PLAN = {8: ((4, -1, 0, 3, -3, 2, -2, 1), (0, 1), (0, -1))}
+PLAN = {8: ((-1, 0, 4, 2, -3, 3, -2, 1), (0, 1), (0, -1))}
 FLOW = (
+    ("shared", 1, 1, 1),
+    ("mix", 1, 1, 12),
     ("near", 1, 1, 1),
-    ("sum1", 1, 1, 5),
-    ("routed", 1, 1, 4),
-    ("slots", 8, 1, 0),
-    ("mix", 3, 2, 11),
+    ("slots", 4, 1, 0),
     ("far", 1, 1, 2),
     ("core", 1, 1, 3),
-    ("shared", 1, 1, 0),
-    ("sum3", 1, 1, 6),
-    ("sum2", 1, 1, 5),
+    ("routed", 1, 1, 4),
+    ("sum3", 1, 1, 8),
+    ("sum1", 1, 1, 5),
+    ("sum2", 1, 1, 6),
 )
 
 

time: 88.8 us -> 87 us (0.980)
  Pallas kernels: 86.2 us -> 85.3 us
    pallas_call x1, Pallas kernels: 86.2 us -> 85.3 us  [layer(): pl.pallas_call(functools.partial(kernel, nz, ny, routes.shape[0]), out_sh...]
where the time goes in v4:
time: 87 us; the launch traced here: 86.9 us
  Pallas kernels  85.3 us (98%)
  local copies, waits for them, and re-layouts  1.57 us (2%)
    pallas_call x1, Pallas kernels, layer(): pl.pallas_call(functools.partial(kernel, nz, ny, routes.shape[0]), out_sh...  85.3 us

profile of v4, /device:TPU:6, one launch (start us, length us, event | category | flops | bytes accessed | tf_op | source)
XLA Modules:
  0.0 86.9 jit_solution(6529202940173155258)
XLA Ops:
  0.0 85.3 %shard_map.91 = bf16[256,256]{1,0:T(8,128)(2,1)} custom-call(bf16[256,2048]{1,0:T(8,128)(2,1)} %tokens_h.1, s32[6,256]{1,0:T(8,128)} %bitcast.10, f32[6,256]{1,0:T(8,128)} %bitcast.11, bf16[2,176,2048]{2,1,0:T(8,128)(2,1)} %bitcast.6, bf16[2,176,2048]{2,1,0:T(8,128)(2,1)} %bitcast.7, bf16[2,176,2048]{2,1,0:T(8,128)(2,1)} %wd_h.1, bf16[352,2048]{1,0:T(8,128)(2,1)} %bitcast.8, ...), custom_call_target="tpu_custom_call" | custom-call | flops 7000000000 | bytes 12000000 | tf_op jit(solution)/shard_map/pallas_call | solution.py:463
  85.3 1.6 %copy.11 = bf16[256,256]{1,0:T(8,128)(2,1)} copy(bf16[256,256]{1,0:T(8,128)(2,1)} %shard_map.91) | data formatting | bytes 262144
